TPU v7x, 128 devices: a whole 4x4x4 slice. The times are simulated.
128 devices in a mesh: pts: 16 (over z, y_hi, core), grp: 8 (over x, y_lo).
Axes of the slice: x: 4, y: 4 (y_hi: 2, y_lo: 2; y = y_hi * 2 + y_lo), z: 4, core: 2. Of those that a mesh axis runs over, the one named last changes fastest.
Arguments:
- adjoint_in: bfloat16 [1152, 1280, 256], P(None, ('pts', 'grp')), may hold values from -6 to 6
- land_sea: int32 [1280, 256], P(('pts', 'grp')), may hold values 0 or 1
- depth_class: int32 [1280, 256], P(('pts', 'grp')), may hold values from 0 to 7
- damping: float32 [1280, 256], P(('pts', 'grp')), may hold values from 0.05 to 0.5
- transparency: float32 [1280, 256], P(('pts', 'grp')), may hold values from 0.6 to 1
- outlets: int32 [64], replicated, may hold values from 0 to 327679
- flux_weight: float32 [1152], replicated, may hold values from 0.5 to 2
- jacobian: bfloat16 [1152, 1152], replicated, may hold values from -0.1875 to 0.1875
- source_scale: float32 [8], replicated, may hold values from 0.1 to 0.5
- freq_damp: float32 [1152], replicated, may hold values from 0.2 to 1
- courant: float32 [32], replicated, may hold values from 0.3 to 0.45
- wind_growth: float32 [1152], replicated, may hold values from 0.01 to 0.06
Outputs:
- adjoint_out: bfloat16 [1152, 1280, 256], P(None, ('pts', 'grp'))
- wind_sens: float32 [2, 1280, 256], P(None, ('pts', 'grp'))
All inputs are finite; a program needn't handle non-finite values. No bound on the sum of `land_sea` on one device may be relied on, other than what follows from the above.
Results may differ from a plain program's by a relative error of at most 0.0057.
Values may be sent and summed in bfloat16 or wider, within the bound.
No kernel may reach another device: no remote copies, remote signals or barrier semaphores. Data moves between devices by JAX's collectives and lax.ppermute only.
A program may use at most 128 MiB of HBM per device.

v0:
```python
import math
import jax
import jax.numpy as jnp
from jax import lax
from jax.sharding import PartitionSpec as P

DIR = 36
FREQ = 32
NSUB = 4
NCLASS = 8


def direction_cosines():
    angles = 2.0 * math.pi * (jnp.arange(DIR, dtype=jnp.float32) + 0.5) / DIR
    return (jnp.tile(jnp.cos(angles), FREQ), jnp.tile(jnp.sin(angles), FREQ))


def upwind_weights(courant):
    cosine, sine = direction_cosines()
    speed = jnp.repeat(courant, DIR)
    along_x = speed * cosine
    along_y = speed * sine
    zeros = jnp.zeros_like(along_x)
    return (
        jnp.maximum(along_x, zeros),
        jnp.maximum(-along_x, zeros),
        jnp.maximum(along_y, zeros),
        jnp.maximum(-along_y, zeros),
        1.0 - jnp.abs(along_x) - jnp.abs(along_y),
    )


def propagate(spectrum, weights, passage):
    eastward, westward, northward, southward, centre_keep = tuple(
        (piece[:, None, None] for piece in weights)
    )
    for substep in range(NSUB):
        padded = jnp.pad(spectrum, ((0, 0), (1, 1), (1, 1)))
        spectrum = passage * (
            centre_keep * spectrum
            + eastward * padded[:, 1:-1, 2:]
            + westward * padded[:, 1:-1, :-2]
            + northward * padded[:, 2:, 1:-1]
            + southward * padded[:, :-2, 1:-1]
        )
    return spectrum


def source_adjoint(spectrum, jacobian, source_rate, damp_rows, freq_damp):
    coupled = lax.dot_general(
        jacobian, spectrum, (((0,), (0,)), ((), ())), preferred_element_type=jnp.float32
    )
    values = spectrum.astype(jnp.float32)
    return (
        values + source_rate[None, :] * coupled - damp_rows[None, :] * freq_damp[:, None] * values
    ).astype(jnp.bfloat16)


def body(
    adjoint_in,
    land_sea,
    depth_class,
    damping,
    transparency,
    outlets,
    flux_weight,
    jacobian,
    source_scale,
    freq_damp,
    courant,
    wind_growth,
):
    components, row_count, lon_count = adjoint_in.shape
    devices = lax.axis_size(("pts", "grp"))
    per_device = components // devices
    point_count = row_count * lon_count
    position = lax.axis_index(("pts", "grp"))
    ocean_local = land_sea.astype(jnp.float32)
    passage_local = ocean_local * transparency
    coastline = lax.all_gather(passage_local, ("pts", "grp"), axis=0, tiled=True)
    cosine, sine = direction_cosines()
    forcing = jnp.stack([wind_growth * cosine, wind_growth * sine])
    ocean_rows = ocean_local.reshape(point_count)
    classes = depth_class.reshape(point_count)
    class_ids = jnp.arange(NCLASS, dtype=jnp.int32)[:, None]
    source_rate = jnp.sum(
        jnp.where(classes[None, :] == class_ids, source_scale[:, None], 0.0), axis=0
    )
    damp_rows = damping.reshape(point_count)
    flat_index = position * point_count + jnp.arange(point_count, dtype=jnp.int32)
    seed_count = jnp.sum((flat_index[None, :] == outlets[:, None]).astype(jnp.float32), axis=0)
    incoming = adjoint_in.reshape(components, point_count)
    seeded = (
        ocean_rows[None, :]
        * (incoming.astype(jnp.float32) + flux_weight[:, None] * seed_count[None, :])
    ).astype(jnp.bfloat16)
    mixed = source_adjoint(seeded, jacobian, source_rate, damp_rows, freq_damp)
    wind_first = jnp.dot(
        forcing, seeded, precision=lax.Precision.HIGHEST, preferred_element_type=jnp.float32
    )
    arrived = lax.all_to_all(
        mixed.reshape(components, row_count, lon_count),
        ("pts", "grp"),
        split_axis=0,
        concat_axis=1,
        tiled=True,
    )
    offset = position * per_device
    local_weights = tuple(
        (
            lax.dynamic_slice_in_dim(piece, offset, per_device, 0)
            for piece in upwind_weights(courant)
        )
    )
    propagated = propagate(arrived.astype(jnp.float32), local_weights, coastline).astype(
        jnp.bfloat16
    )
    home = lax.all_to_all(
        propagated, ("pts", "grp"), split_axis=1, concat_axis=0, tiled=True
    ).reshape(components, point_count)
    adjoint_out = source_adjoint(home, jacobian, source_rate, damp_rows, freq_damp).reshape(
        components, row_count, lon_count
    )
    wind_second = jnp.dot(
        forcing, home, precision=lax.Precision.HIGHEST, preferred_element_type=jnp.float32
    )
    wind_sens = (wind_first + wind_second).reshape(2, row_count, lon_count)
    return (adjoint_out, wind_sens)


def solution(mesh):
    placed = (
        P(None, ("pts", "grp"), None),
        P(("pts", "grp"), None),
        P(("pts", "grp"), None),
        P(("pts", "grp"), None),
        P(("pts", "grp"), None),
        P(),
        P(),
        P(),
        P(),
        P(),
        P(),
        P(),
    )
    return jax.shard_map(
        body,
        mesh=mesh,
        in_specs=placed,
        out_specs=(P(None, ("pts", "grp"), None), P(None, ("pts", "grp"), None)),
        check_vma=False,
    )
```

profile of v0, /device:TPU:2, one launch (start us, length us, event | category | flops | bytes accessed | tf_op | source)
XLA Modules:
  0.0 821.9 jit_solution(16402472275892524580)
XLA Ops:
  7.2 0.0 copy-start
  7.2 0.0 copy-start.7
  7.2 0.0 copy-start.8
  7.2 0.9 mul.129
  8.1 0.7 eq.31
  8.8 0.7 convert_element_type.47
  9.5 9.9 %copy.44 = f32[1152,10,256]{0,2,1:T(8,128)} copy(bf16[1152,10,256]{2,0,1:T(8,128)(2,1)} %param.12) | data formatting | bytes 17694720 | tf_op jit(solution)/shard_map/convert_element_type | solution.py:95
  19.4 0.2 convert_reduce_fusion
  19.6 0.1 select_reduce_fusion
  19.7 5.8 fusion.42
  25.5 0.0 copy-done
  25.5 0.0 copy-done.10
  25.6 0.0 copy-start.2
  25.6 10.9 %fusion.44 = bf16[1152,2560]{0,1:T(8,128)(2,1)} fusion(bf16[1152,2560]{0,1:T(8,128)(2,1)S(1)} %fusion.42, bf16[1152,1152]{1,0:T(8,128)(2,1)S(1)} %copy-done, f32[1152]{0:T(1024)S(1)} %copy-done.10, f32[2560]{0:T(1024)S(1)} %mul.129, f32[2560]{0:T(1024)S(1)} %select_reduce_fusion), kind=kOutput, calls=%fused_computation.67 | convolution fusion | flops 6815416320 | bytes 14475776 | tf_op jit(solution)/shard_map/dot_general | solution.py:50
  36.4 12.0 %copy.45 = bf16[1152,10,256]{2,1,0:T(8,128)(2,1)} copy(bf16[1152,10,256]{0,2,1:T(8,128)(2,1)} %bitcast.49) | data formatting | bytes 11796480 | tf_op jit(solution)/shard_map/reshape | solution.py:102
  48.5 10.9 %all-to-all-start = ((bf16[1152,10,256]{2,1,0:T(8,128)(2,1)}), bf16[1152,10,256]{2,1,0:T(8,128)(2,1)}, u32[]{:S(2)}, u32[]{:S(2)}) async-start(bf16[1152,10,256]{2,1,0:T(8,128)(2,1)} %copy.45), calls=%async_computation | async-start | bytes 18874368 | tf_op jit(solution)/shard_map/all_to_all | solution.py:101
  59.4 0.4 all-gather.3.cloned.1.call-start
  59.8 0.0 copy-done.3
  59.9 0.0 copy-done.4
  59.9 0.6 multiply_bitcast_fusion
  60.5 0.0 all-gather.3.cloned.1.call-update
  60.6 0.1 tile.19
  60.7 0.1 tile.17
  60.8 0.1 broadcast_in_dim.16
  60.9 0.1 reshape.55
  61.0 0.1 abs_subtract_fusion
  61.1 365.3 %all-gather.3.cloned.1.call-done = f32[128,10,256]{2,1,0:T(8,128)} async-done(((f32[1,10,256]{2,1,0:T(8,128)}), f32[128,10,256]{2,1,0:T(8,128)}) %all-gather.3.cloned.1.call-update) | async-done | bytes 1310736 | tf_op jit(solution)/shard_map/all_gather | solution.py:80
  426.5 2.5 reshape.64
  429.0 0.0 all-to-all-done
  429.0 9.9 %copy_convert_fusion = f32[1152,10,256]{2,0,1:T(8,128)} fusion(bf16[1152,10,256]{2,1,0:T(8,128)(2,1)} %all-to-all-done), kind=kLoop, calls=%fused_computation.68 | loop fusion | flops 2949120 | bytes 17694720 | tf_op jit(solution)/shard_map/convert_element_type | solution.py:115
  438.8 15.4 %reshape.62 = f32[128,9,10,256]{3,1,0,2:T(8,128)} reshape(f32[1152,10,256]{2,0,1:T(8,128)} %copy_convert_fusion) | data formatting | bytes 23592960 | tf_op jit(solution)/shard_map/convert_element_type | solution.py:115
  454.2 19.6 %copy.47 = f32[9,128,10,256]{3,2,1,0:T(8,128)} copy(f32[9,128,10,256]{3,0,1,2:T(8,128)} %bitcast.43) | data formatting | bytes 23592960 | tf_op jit(solution)/shard_map/convert_element_type | solution.py:115
  473.8 16.4 %reshape.61 = f32[9,1280,256]{2,1,0:T(8,128)} reshape(f32[9,128,10,256]{3,2,1,0:T(8,128)} %copy.47) | data formatting | bytes 23592960 | tf_op jit(solution)/shard_map/convert_element_type | solution.py:115
  490.2 25.7 %fusion.9 = f32[9,1280,256]{2,1,0:T(8,128)} fusion(f32[9,1280,256]{2,1,0:T(8,128)} %reshape.61, f32[9]{0:T(128)S(1)} %get-tuple-element.20, f32[9]{0:T(128)S(1)} %get-tuple-element.19, f32[9]{0:T(128)S(1)} %get-tuple-element.17, f32[9]{0:T(128)S(1)} %get-tuple-element.18, f32[9]{0:T(128)S(1)} %get-tuple-element.16, f32[1280,256]{1,0:T(8,128)} %reshape.64), kind=kLoop, calls=%fused_computation.31 | loop fusion | flops 29491200 | bytes 24903860 | tf_op jit(solution)/shard_map/mul | solution.py:39
  515.9 0.0 copy-done.1
  515.9 25.3 %fusion.18 = f32[9,1280,256]{2,1,0:T(8,128)} fusion(f32[9,1280,256]{2,1,0:T(8,128)} %fusion.9, f32[9]{0:T(128)S(1)} %get-tuple-element.20, f32[9]{0:T(128)S(1)} %get-tuple-element.19, f32[9]{0:T(128)S(1)} %get-tuple-element.17, f32[9]{0:T(128)S(1)} %get-tuple-element.18, f32[9]{0:T(128)S(1)} %get-tuple-element.16, f32[1280,256]{1,0:T(8,128)S(1)} %copy-done.1), kind=kLoop, calls=%fused_computation.40 | loop fusion | flops 29491200 | bytes 24903860 | tf_op jit(solution)/shard_map/mul | solution.py:39
  541.2 25.3 %fusion.27 = f32[9,1280,256]{2,1,0:T(8,128)} fusion(f32[9,1280,256]{2,1,0:T(8,128)} %fusion.18, f32[9]{0:T(128)S(1)} %get-tuple-element.20, f32[9]{0:T(128)S(1)} %get-tuple-element.19, f32[9]{0:T(128)S(1)} %get-tuple-element.17, f32[9]{0:T(128)S(1)} %get-tuple-element.18, f32[9]{0:T(128)S(1)} %get-tuple-element.16, f32[1280,256]{1,0:T(8,128)S(1)} %copy-done.1), kind=kLoop, calls=%fused_computation.49 | loop fusion | flops 29491200 | bytes 24903860 | tf_op jit(solution)/shard_map/mul | solution.py:39
  566.6 34.8 %fusion.37 = bf16[9,1280,256]{2,1,0:T(8,128)(2,1)} fusion(f32[9,1280,256]{2,1,0:T(8,128)} %fusion.27, f32[9]{0:T(128)S(1)} %get-tuple-element.20, f32[9]{0:T(128)S(1)} %get-tuple-element.19, f32[9]{0:T(128)S(1)} %get-tuple-element.17, f32[9]{0:T(128)S(1)} %get-tuple-element.18, f32[9]{0:T(128)S(1)} %get-tuple-element.16, f32[1280,256]{1,0:T(8,128)S(1)} %copy-done.1), kind=kLoop, calls=%fused_computation.59 | loop fusion | flops 32440320 | bytes 19005620 | tf_op jit(solution)/shard_map/convert_element_type | solution.py:115
  601.4 9.5 %copy.48 = bf16[9,1280,256]{2,0,1:T(8,128)(2,1)} copy(bf16[9,1280,256]{2,1,0:T(8,128)(2,1)} %fusion.37) | data formatting | bytes 11796480 | tf_op jit(solution)/shard_map/convert_element_type | solution.py:115
  610.9 9.3 %all-to-all-start.1 = ((bf16[9,1280,256]{2,0,1:T(8,128)(2,1)}), bf16[9,1280,256]{2,0,1:T(8,128)(2,1)}, u32[]{:S(2)}, u32[]{:S(2)}) async-start(bf16[9,1280,256]{2,0,1:T(8,128)(2,1)} %copy.48), calls=%async_computation.1 | async-start | bytes 20971520 | tf_op jit(solution)/shard_map/all_to_all | solution.py:118
  620.2 7.3 fusion.45
  627.5 126.8 %all-to-all-done.1 = bf16[9,1280,256]{2,0,1:T(8,128)(2,1)} async-done(((bf16[9,1280,256]{2,0,1:T(8,128)(2,1)}), bf16[9,1280,256]{2,0,1:T(8,128)(2,1)}, u32[]{:S(2)}, u32[]{:S(2)}) %all-to-all-start.1) | async-done | bytes 5898272 | tf_op jit(solution)/shard_map/all_to_all | solution.py:118
  754.3 12.1 %copy.50 = bf16[128,9,10,256]{3,2,1,0:T(8,128)(2,1)} copy(bf16[128,9,10,256]{3,1,2,0:T(8,128)(2,1)} %bitcast.7) | data formatting | bytes 11796480 | tf_op jit(solution)/shard_map/all_to_all | solution.py:118
  766.4 10.2 %copy.56 = bf16[144,8,10,256]{3,1,2,0:T(8,128)(2,1)} copy(bf16[144,8,10,256]{3,2,1,0:T(8,128)(2,1)} %bitcast.47) | data formatting | bytes 11796480
  776.6 8.8 %copy.51 = bf16[1152,2560]{0,1:T(8,128)(2,1)} copy(bf16[1152,2560]{1,0:T(8,128)(2,1)} %bitcast.44) | data formatting | bytes 11796480 | tf_op jit(solution)/shard_map/reshape | solution.py:120
  785.5 5.7 convolution_add_fusion
  791.1 14.8 %fusion.43 = bf16[1152,2560]{0,1:T(8,128)(2,1)} fusion(bf16[1152,2560]{0,1:T(8,128)(2,1)} %copy.51, bf16[1152,2560]{1,0:T(8,128)(2,1)} %bitcast.46, bf16[1152,1152]{1,0:T(8,128)(2,1)S(1)} %copy-done, f32[1152]{0:T(1024)S(1)} %copy-done.10, f32[2560]{0:T(1024)S(1)} %mul.129, f32[2560]{0:T(1024)S(1)} %select_reduce_fusion), kind=kOutput, calls=%fused_computation.66 | convolution fusion | flops 6815416320 | bytes 20374016 | tf_op jit(solution)/shard_map/dot_general | solution.py:50
  806.0 8.9 %copy.52 = bf16[1152,10,256]{2,0,1:T(8,128)(2,1)} copy(bf16[1152,10,256]{0,2,1:T(8,128)(2,1)} %bitcast.48) | data formatting | bytes 11796480
  (22 shorter events, 0.2 us)
Async XLA Ops:
  7.2 18.4 %copy-start = (bf16[1152,1152]{1,0:T(8,128)(2,1)S(1)}, bf16[1152,1152]{1,0:T(8,128)(2,1)}, u32[]{:S(2)}) copy-start(bf16[1152,1152]{1,0:T(8,128)(2,1)} %param.19) | copy-start | bytes 7962628
  7.2 12.3 %copy-start.7 = (s32[64]{0:T(128)S(1)}, s32[64]{0:T(128)}, u32[]{:S(2)}) copy-start(s32[64]{0:T(128)} %param.17) | copy-start | bytes 772
  7.2 12.4 %copy-start.8 = (f32[8]{0:T(128)S(1)}, f32[8]{0:T(128)}, u32[]{:S(2)}) copy-start(f32[8]{0:T(128)} %param.20) | copy-start | bytes 100
  7.2 12.5 %copy-start.5 = (f32[1152]{0:T(1024)S(1)}, f32[1152]{0:T(1024)}, u32[]{:S(2)}) copy-start(f32[1152]{0:T(1024)} %param.18) | copy-start | bytes 13828
  19.4 6.1 copy-start.10
  25.6 10.9 %copy-start.2 = (bf16[1152,2560]{0,1:T(8,128)(2,1)}, bf16[1152,2560]{0,1:T(8,128)(2,1)S(1)}, u32[]{:S(2)}) copy-start(bf16[1152,2560]{0,1:T(8,128)(2,1)S(1)} %fusion.42) | copy-start | bytes 17694724
  48.5 11.4 %copy-start.3 = (s32[10,256]{1,0:T(8,128)S(1)}, s32[10,256]{1,0:T(8,128)}, u32[]{:S(2)}) copy-start(s32[10,256]{1,0:T(8,128)} %param.13) | copy-start | bytes 30724
  48.5 11.4 %copy-start.4 = (f32[10,256]{1,0:T(8,128)S(1)}, f32[10,256]{1,0:T(8,128)}, u32[]{:S(2)}) copy-start(f32[10,256]{1,0:T(8,128)} %param.16) | copy-start | bytes 30724
  48.5 12.4 %copy-start.9 = (f32[32]{0:T(128)S(1)}, f32[32]{0:T(128)}, u32[]{:S(2)}) copy-start(f32[32]{0:T(128)} %param.22) | copy-start | bytes 388
  48.5 12.5 %copy-start.6 = (f32[1152]{0:T(1024)S(1)}, f32[1152]{0:T(1024)}, u32[]{:S(2)}) copy-start(f32[1152]{0:T(1024)} %param.23) | copy-start | bytes 13828
  48.5 380.5 %all-to-all-start = ((bf16[1152,10,256]{2,1,0:T(8,128)(2,1)}), bf16[1152,10,256]{2,1,0:T(8,128)(2,1)}, u32[]{:S(2)}, u32[]{:S(2)}) async-start(bf16[1152,10,256]{2,1,0:T(8,128)(2,1)} %copy.45), calls=%async_computation | async-start | bytes 18874368 | tf_op jit(solution)/shard_map/all_to_all | solution.py:101
  59.4 367.0 %all-gather.3.cloned.1.call-start = ((), (), s32[]{:S(2)}) async-start(), calls=%async_computation.2 | async-start | bytes 2113536 | tf_op jit(solution)/shard_map/all_gather | solution.py:80
  490.2 25.7 %copy-start.1 = (f32[1280,256]{1,0:T(8,128)S(1)}, f32[1280,256]{1,0:T(8,128)}, u32[]{:S(2)}) copy-start(f32[1280,256]{1,0:T(8,128)} %reshape.64) | copy-start | bytes 3932164
  610.9 143.4 %all-to-all-start.1 = ((bf16[9,1280,256]{2,0,1:T(8,128)(2,1)}), bf16[9,1280,256]{2,0,1:T(8,128)(2,1)}, u32[]{:S(2)}, u32[]{:S(2)}) async-start(bf16[9,1280,256]{2,0,1:T(8,128)(2,1)} %copy.48), calls=%async_computation.1 | async-start | bytes 20971520 | tf_op jit(solution)/shard_map/all_to_all | solution.py:118
Sparse Core Ops, SparseCore 0:
  62.5 363.9 all-gather.2
where the time goes:
time: 828 us; the launch traced here: 822 us
  waiting for transfers between devices  492 us (59%)
  other arithmetic  129 us (16%)
  local copies, waits for them, and re-layouts  127 us (15%)
  matrix products  38.7 us (5%)
  starting transfers between devices  20.6 us (2%)
  between operations  14.5 us (2%)
    all_gather x1, waiting for transfers between devices, body(): lax.all_gather(passage_local, ('pts', 'grp'), axis=0, tiled=True)  365 us
    all_to_all x1, waiting for transfers between devices, body(): lax.all_to_all(propagated, ('pts', 'grp'), split_axis=1, concat_axis=0, t...  127 us
    mul x3, other arithmetic, propagate(): passage * (centre_keep * spectrum + eastward * padded[:, 1:-1, 2:] + west...  76.3 us
    convert_element_type x3, local copies, waits for them, and re-layouts, body(): arrived.astype(jnp.float32)  51.4 us
    convert_element_type x1, other arithmetic, body(): propagate(arrived.astype(jnp.float32), local_weights, coastline)  34.8 us
    dot_general x2, matrix products, source_adjoint(): lax.dot_general(jacobian, spectrum, (((0,), (0,)), ((), ())), preferred_e...  25.7 us
    unnamed x25, local copies, waits for them, and re-layouts  21.6 us
  transfers between devices with their start and end apart: 3, of which 2 were waited for; matrix products, arithmetic and copies ran while one was open for 1% of the time, Pallas kernels for 0%

commit v1 on v0

--- a/solution.py
+++ b/solution.py
@@ -77,7 +77,8 @@
     position = lax.axis_index(("pts", "grp"))
     ocean_local = land_sea.astype(jnp.float32)
     passage_local = ocean_local * transparency
-    coastline = lax.all_gather(passage_local, ("pts", "grp"), axis=0, tiled=True)
+    repeated = jnp.stack([passage_local] * lax.axis_size(("pts", "grp")))
+    coastline = jnp.concatenate(lax.all_to_all(repeated, ("pts", "grp"), 0, 0), axis=0)
     cosine, sine = direction_cosines()
     forcing = jnp.stack([wind_growth * cosine, wind_growth * sine])
     ocean_rows = ocean_local.reshape(point_count)

time: 828 us -> 576 us (0.70)
  waiting for transfers between devices: 492 us -> 243 us
  between operations: 14.5 us -> 1.05 us
    all_gather x1 -> x0, waiting for transfers between devices: 365 us -> none  [body(): lax.all_gather(passage_local, ('pts', 'grp'), axis=0, tiled=True)]
    all_to_all x1, waiting for transfers between devices: 0.01 us -> 116 us  [body(): lax.all_to_all(mixed.reshape(components, row_count, lon_count), ('pts', '...]
    all_to_all x0 -> x1, starting transfers between devices: none -> 11 us  [body(): lax.all_to_all(repeated, ('pts', 'grp'), 0, 0)]
    unnamed x25 -> x20, local copies, waits for them, and re-layouts: 21.6 us -> 19.1 us
  transfers between devices with their start and end apart: 3 -> 3, of which waited for: 2 -> 2; matrix products, arithmetic and copies ran while one was open for 1% -> 9% of each run, Pallas kernels for 0% -> 0%
where the time goes in v1:
time: 576 us; the launch traced here: 569 us
  waiting for transfers between devices  243 us (42%)
  local copies, waits for them, and re-layouts  129 us (22%)
  other arithmetic  129 us (22%)
  matrix products  38.7 us (7%)
  starting transfers between devices  28.1 us (5%)
    all_to_all x1, waiting for transfers between devices, body(): lax.all_to_all(propagated, ('pts', 'grp'), split_axis=1, concat_axis=0, t...  127 us
    all_to_all x1, waiting for transfers between devices, body(): lax.all_to_all(mixed.reshape(components, row_count, lon_count), ('pts', '...  116 us
    mul x3, other arithmetic, propagate(): passage * (centre_keep * spectrum + eastward * padded[:, 1:-1, 2:] + west...  76.2 us
    convert_element_type x3, local copies, waits for them, and re-layouts, body(): arrived.astype(jnp.float32)  51.4 us
    convert_element_type x1, other arithmetic, body(): propagate(arrived.astype(jnp.float32), local_weights, coastline)  34.8 us
    dot_general x2, matrix products, source_adjoint(): lax.dot_general(jacobian, spectrum, (((0,), (0,)), ((), ())), preferred_e...  25.7 us
    unnamed x20, local copies, waits for them, and re-layouts  19.1 us
    all_to_all x1, local copies, waits for them, and re-layouts, body(): lax.all_to_all(propagated, ('pts', 'grp'), split_axis=1, concat_axis=0, t...  12.1 us
  transfers between devices with their start and end apart: 3, of which 2 were waited for; matrix products, arithmetic and copies ran while one was open for 9% of the time, Pallas kernels for 0%

profile of v1, /device:TPU:2, one launch (start us, length us, event | category | flops | bytes accessed | tf_op | source)
XLA Modules:
  0.0 568.7 jit_solution(18182555580563825384)
XLA Ops:
  0.6 0.0 copy-start
  0.6 0.9 convert_multiply_fusion
  1.5 0.0 copy-start.3
  1.6 1.6 stack.8
  3.1 11.0 %all-to-all-start = ((f32[128,10,256]{2,1,0:T(8,128)}), f32[128,10,256]{2,1,0:T(8,128)}, u32[]{:S(2)}, u32[]{:S(2)}) async-start(f32[128,10,256]{2,1,0:T(8,128)} %stack.8), calls=%async_computation | async-start | bytes 4194304 | tf_op jit(solution)/shard_map/all_to_all | solution.py:81
  14.1 0.7 convert_element_type.47
  14.9 0.7 mul.132
  15.6 0.7 eq.31
  16.3 9.9 %copy.44 = f32[1152,10,256]{0,2,1:T(8,128)} copy(bf16[1152,10,256]{2,0,1:T(8,128)(2,1)} %param.12) | data formatting | bytes 17694720 | tf_op jit(solution)/shard_map/convert_element_type | solution.py:96
  26.2 0.0 copy-done.5
  26.2 0.2 convert_reduce_fusion
  26.3 0.0 copy-done.6
  26.3 0.1 select_reduce_fusion
  26.4 0.0 copy-done.3
  26.5 5.8 %fusion.42 = bf16[1152,2560]{0,1:T(8,128)(2,1)S(1)} fusion(f32[1152,10,256]{0,2,1:T(8,128)} %copy.44, f32[2560]{0:T(1024)S(1)} %convert_reduce_fusion, f32[1152]{0:T(1024)S(1)} %copy-done.3, f32[2560]{0:T(1024)S(1)} %mul.122), kind=kLoop, calls=%fused_computation.65 | loop fusion | flops 11796480 | bytes 17719808 | tf_op jit(solution)/shard_map/convert_element_type | solution.py:97
  32.3 0.0 copy-done
  32.3 0.0 copy-done.8
  32.3 0.0 copy-start.2
  32.3 10.9 %fusion.44 = bf16[1152,2560]{0,1:T(8,128)(2,1)} fusion(bf16[1152,2560]{0,1:T(8,128)(2,1)S(1)} %fusion.42, bf16[1152,1152]{1,0:T(8,128)(2,1)S(1)} %copy-done, f32[1152]{0:T(1024)S(1)} %copy-done.8, f32[2560]{0:T(1024)S(1)} %mul.132, f32[2560]{0:T(1024)S(1)} %select_reduce_fusion), kind=kOutput, calls=%fused_computation.67 | convolution fusion | flops 6815416320 | bytes 14475776 | tf_op jit(solution)/shard_map/dot_general | solution.py:50
  43.2 12.0 %copy.45 = bf16[1152,10,256]{2,1,0:T(8,128)(2,1)} copy(bf16[1152,10,256]{0,2,1:T(8,128)(2,1)} %bitcast.47) | data formatting | bytes 11796480 | tf_op jit(solution)/shard_map/reshape | solution.py:103
  55.2 0.0 all-to-all-done
  55.2 10.7 %all-to-all-start.1 = ((bf16[1152,10,256]{2,1,0:T(8,128)(2,1)}), bf16[1152,10,256]{2,1,0:T(8,128)(2,1)}, u32[]{:S(2)}, u32[]{:S(2)}) async-start(bf16[1152,10,256]{2,1,0:T(8,128)(2,1)} %copy.45), calls=%async_computation.1 | async-start | bytes 18874368 | tf_op jit(solution)/shard_map/all_to_all | solution.py:102
  66.0 0.1 tile.19
  66.2 0.1 tile.17
  66.3 0.1 broadcast_in_dim.16
  66.4 0.1 reshape.57
  66.5 0.0 copy-done.4
  66.5 0.1 abs_subtract_fusion
  66.6 2.5 mul.115
  69.1 116.5 %all-to-all-done.1 = bf16[1152,10,256]{2,1,0:T(8,128)(2,1)} async-done(((bf16[1152,10,256]{2,1,0:T(8,128)(2,1)}), bf16[1152,10,256]{2,1,0:T(8,128)(2,1)}, u32[]{:S(2)}, u32[]{:S(2)}) %all-to-all-start.1) | async-done | bytes 5898272 | tf_op jit(solution)/shard_map/all_to_all | solution.py:102
  185.5 9.9 %copy_convert_fusion = f32[1152,10,256]{2,0,1:T(8,128)} fusion(bf16[1152,10,256]{2,1,0:T(8,128)(2,1)} %all-to-all-done.1), kind=kLoop, calls=%fused_computation.68 | loop fusion | flops 2949120 | bytes 17694720 | tf_op jit(solution)/shard_map/convert_element_type | solution.py:116
  195.4 15.4 %reshape.64 = f32[128,9,10,256]{3,1,0,2:T(8,128)} reshape(f32[1152,10,256]{2,0,1:T(8,128)} %copy_convert_fusion) | data formatting | bytes 23592960 | tf_op jit(solution)/shard_map/convert_element_type | solution.py:116
  210.8 19.6 %copy.47 = f32[9,128,10,256]{3,2,1,0:T(8,128)} copy(f32[9,128,10,256]{3,0,1,2:T(8,128)} %bitcast.41) | data formatting | bytes 23592960 | tf_op jit(solution)/shard_map/convert_element_type | solution.py:116
  230.4 16.4 %reshape.63 = f32[9,1280,256]{2,1,0:T(8,128)} reshape(f32[9,128,10,256]{3,2,1,0:T(8,128)} %copy.47) | data formatting | bytes 23592960 | tf_op jit(solution)/shard_map/convert_element_type | solution.py:116
  246.8 25.7 %fusion.9 = f32[9,1280,256]{2,1,0:T(8,128)} fusion(f32[9,1280,256]{2,1,0:T(8,128)} %reshape.63, f32[9]{0:T(128)S(1)} %get-tuple-element.20, f32[9]{0:T(128)S(1)} %get-tuple-element.19, f32[9]{0:T(128)S(1)} %get-tuple-element.17, f32[9]{0:T(128)S(1)} %get-tuple-element.18, f32[9]{0:T(128)S(1)} %get-tuple-element.16, f32[1280,256]{1,0:T(8,128)} %mul.115), kind=kLoop, calls=%fused_computation.31 | loop fusion | flops 29491200 | bytes 24903860 | tf_op jit(solution)/shard_map/mul | solution.py:39
  272.5 25.3 %fusion.18 = f32[9,1280,256]{2,1,0:T(8,128)} fusion(f32[9,1280,256]{2,1,0:T(8,128)} %fusion.9, f32[9]{0:T(128)S(1)} %get-tuple-element.20, f32[9]{0:T(128)S(1)} %get-tuple-element.19, f32[9]{0:T(128)S(1)} %get-tuple-element.17, f32[9]{0:T(128)S(1)} %get-tuple-element.18, f32[9]{0:T(128)S(1)} %get-tuple-element.16, f32[1280,256]{1,0:T(8,128)S(1)} %copy-done.1), kind=kLoop, calls=%fused_computation.40 | loop fusion | flops 29491200 | bytes 24903860 | tf_op jit(solution)/shard_map/mul | solution.py:39
  297.7 25.3 %fusion.27 = f32[9,1280,256]{2,1,0:T(8,128)} fusion(f32[9,1280,256]{2,1,0:T(8,128)} %fusion.18, f32[9]{0:T(128)S(1)} %get-tuple-element.20, f32[9]{0:T(128)S(1)} %get-tuple-element.19, f32[9]{0:T(128)S(1)} %get-tuple-element.17, f32[9]{0:T(128)S(1)} %get-tuple-element.18, f32[9]{0:T(128)S(1)} %get-tuple-element.16, f32[1280,256]{1,0:T(8,128)S(1)} %copy-done.1), kind=kLoop, calls=%fused_computation.49 | loop fusion | flops 29491200 | bytes 24903860 | tf_op jit(solution)/shard_map/mul | solution.py:39
  323.0 34.8 %fusion.37 = bf16[9,1280,256]{2,1,0:T(8,128)(2,1)} fusion(f32[9,1280,256]{2,1,0:T(8,128)} %fusion.27, f32[9]{0:T(128)S(1)} %get-tuple-element.20, f32[9]{0:T(128)S(1)} %get-tuple-element.19, f32[9]{0:T(128)S(1)} %get-tuple-element.17, f32[9]{0:T(128)S(1)} %get-tuple-element.18, f32[9]{0:T(128)S(1)} %get-tuple-element.16, f32[1280,256]{1,0:T(8,128)S(1)} %copy-done.1), kind=kLoop, calls=%fused_computation.59 | loop fusion | flops 32440320 | bytes 19005620 | tf_op jit(solution)/shard_map/convert_element_type | solution.py:116
  357.8 9.5 %copy.48 = bf16[9,1280,256]{2,0,1:T(8,128)(2,1)} copy(bf16[9,1280,256]{2,1,0:T(8,128)(2,1)} %fusion.37) | data formatting | bytes 11796480 | tf_op jit(solution)/shard_map/convert_element_type | solution.py:116
  367.4 6.4 %all-to-all-start.2 = ((bf16[9,1280,256]{2,0,1:T(8,128)(2,1)}), bf16[9,1280,256]{2,0,1:T(8,128)(2,1)}, u32[]{:S(2)}, u32[]{:S(2)}) async-start(bf16[9,1280,256]{2,0,1:T(8,128)(2,1)} %copy.48), calls=%async_computation.2 | async-start | bytes 20971520 | tf_op jit(solution)/shard_map/all_to_all | solution.py:119
  373.8 7.3 %fusion.45 = f32[2,2560]{1,0:T(2,128)S(1)} fusion(bf16[1152,2560]{0,1:T(8,128)(2,1)} %copy-done.2, f32[1,1152]{1,0:T(1,128)S(1)} %stack.10, f32[1,1152]{1,0:T(1,128)S(1)} %stack.9), kind=kOutput, calls=%fused_computation.75 | convolution fusion | flops 70781184 | bytes 5927936 | tf_op jit(solution)/shard_map/dot_general | solution.py:99
  381.1 126.8 %all-to-all-done.2 = bf16[9,1280,256]{2,0,1:T(8,128)(2,1)} async-done(((bf16[9,1280,256]{2,0,1:T(8,128)(2,1)}), bf16[9,1280,256]{2,0,1:T(8,128)(2,1)}, u32[]{:S(2)}, u32[]{:S(2)}) %all-to-all-start.2) | async-done | bytes 5898272 | tf_op jit(solution)/shard_map/all_to_all | solution.py:119
  507.9 12.1 %copy.50 = bf16[128,9,10,256]{3,2,1,0:T(8,128)(2,1)} copy(bf16[128,9,10,256]{3,1,2,0:T(8,128)(2,1)} %bitcast.6) | data formatting | bytes 11796480 | tf_op jit(solution)/shard_map/all_to_all | solution.py:119
  520.0 10.2 %copy.56 = bf16[144,8,10,256]{3,1,2,0:T(8,128)(2,1)} copy(bf16[144,8,10,256]{3,2,1,0:T(8,128)(2,1)} %bitcast.45) | data formatting | bytes 11796480
  530.2 8.9 %copy.51 = bf16[1152,2560]{0,1:T(8,128)(2,1)} copy(bf16[1152,2560]{1,0:T(8,128)(2,1)} %bitcast.42) | data formatting | bytes 11796480 | tf_op jit(solution)/shard_map/reshape | solution.py:121
  539.1 5.7 convolution_add_fusion
  544.7 14.8 %fusion.43 = bf16[1152,2560]{0,1:T(8,128)(2,1)} fusion(bf16[1152,2560]{0,1:T(8,128)(2,1)} %copy.51, bf16[1152,2560]{1,0:T(8,128)(2,1)} %bitcast.44, bf16[1152,1152]{1,0:T(8,128)(2,1)S(1)} %copy-done, f32[1152]{0:T(1024)S(1)} %copy-done.8, f32[2560]{0:T(1024)S(1)} %mul.132, f32[2560]{0:T(1024)S(1)} %select_reduce_fusion), kind=kOutput, calls=%fused_computation.66 | convolution fusion | flops 6815416320 | bytes 20374016 | tf_op jit(solution)/shard_map/dot_general | solution.py:50
  559.6 8.9 %copy.52 = bf16[1152,10,256]{2,0,1:T(8,128)(2,1)} copy(bf16[1152,10,256]{0,2,1:T(8,128)(2,1)} %bitcast.46) | data formatting | bytes 11796480
  (18 shorter events, 0.1 us)
Async XLA Ops:
  0.6 31.6 %copy-start = (bf16[1152,1152]{1,0:T(8,128)(2,1)S(1)}, bf16[1152,1152]{1,0:T(8,128)(2,1)}, u32[]{:S(2)}) copy-start(bf16[1152,1152]{1,0:T(8,128)(2,1)} %param.19) | copy-start | bytes 7962628
  1.5 24.6 %copy-start.5 = (s32[64]{0:T(128)S(1)}, s32[64]{0:T(128)}, u32[]{:S(2)}) copy-start(s32[64]{0:T(128)} %param.17) | copy-start | bytes 772
  1.5 24.8 %copy-start.6 = (f32[8]{0:T(128)S(1)}, f32[8]{0:T(128)}, u32[]{:S(2)}) copy-start(f32[8]{0:T(128)} %param.20) | copy-start | bytes 100
  1.5 24.9 %copy-start.3 = (f32[1152]{0:T(1024)S(1)}, f32[1152]{0:T(1024)}, u32[]{:S(2)}) copy-start(f32[1152]{0:T(1024)} %param.18) | copy-start | bytes 13828
  3.1 52.1 %all-to-all-start = ((f32[128,10,256]{2,1,0:T(8,128)}), f32[128,10,256]{2,1,0:T(8,128)}, u32[]{:S(2)}, u32[]{:S(2)}) async-start(f32[128,10,256]{2,1,0:T(8,128)} %stack.8), calls=%async_computation | async-start | bytes 4194304 | tf_op jit(solution)/shard_map/all_to_all | solution.py:81
  26.2 6.1 %copy-start.8 = (f32[1152]{0:T(1024)S(1)}, f32[1152]{0:T(1024)}, u32[]{:S(2)}) copy-start(f32[1152]{0:T(1024)} %param.21) | copy-start | bytes 13828
  32.3 10.9 %copy-start.2 = (bf16[1152,2560]{0,1:T(8,128)(2,1)}, bf16[1152,2560]{0,1:T(8,128)(2,1)S(1)}, u32[]{:S(2)}) copy-start(bf16[1152,2560]{0,1:T(8,128)(2,1)S(1)} %fusion.42) | copy-start | bytes 17694724
  55.2 11.1 %copy-start.7 = (f32[32]{0:T(128)S(1)}, f32[32]{0:T(128)}, u32[]{:S(2)}) copy-start(f32[32]{0:T(128)} %param.22) | copy-start | bytes 388
  55.2 11.3 %copy-start.4 = (f32[1152]{0:T(1024)S(1)}, f32[1152]{0:T(1024)}, u32[]{:S(2)}) copy-start(f32[1152]{0:T(1024)} %param.23) | copy-start | bytes 13828
  55.2 130.3 %all-to-all-start.1 = ((bf16[1152,10,256]{2,1,0:T(8,128)(2,1)}), bf16[1152,10,256]{2,1,0:T(8,128)(2,1)}, u32[]{:S(2)}, u32[]{:S(2)}) async-start(bf16[1152,10,256]{2,1,0:T(8,128)(2,1)} %copy.45), calls=%async_computation.1 | async-start | bytes 18874368 | tf_op jit(solution)/shard_map/all_to_all | solution.py:102
  246.8 25.7 %copy-start.1 = (f32[1280,256]{1,0:T(8,128)S(1)}, f32[1280,256]{1,0:T(8,128)}, u32[]{:S(2)}) copy-start(f32[1280,256]{1,0:T(8,128)} %mul.115) | copy-start | bytes 3932164
  367.4 140.5 %all-to-all-start.2 = ((bf16[9,1280,256]{2,0,1:T(8,128)(2,1)}), bf16[9,1280,256]{2,0,1:T(8,128)(2,1)}, u32[]{:S(2)}, u32[]{:S(2)}) async-start(bf16[9,1280,256]{2,0,1:T(8,128)(2,1)} %copy.48), calls=%async_computation.2 | async-start | bytes 20971520 | tf_op jit(solution)/shard_map/all_to_all | solution.py:119
